TPU v7x, 128 devices: a whole 4x4x4 slice. The times are simulated.
128 devices in a mesh: sim: 32 (over y_hi, z, x), learn: 4 (over y_lo, core).
Axes of the slice: x: 4, y: 4 (y_hi: 2, y_lo: 2; y = y_hi * 2 + y_lo), z: 4, core: 2. Of those that a mesh axis runs over, the one named last changes fastest.
Arguments:
- fields: float32 [8, 256, 32, 128], P(None, 'sim', 'learn'), may hold values from -2.2 to 2.2
- diffusivity: float32 [8], replicated, may hold values from 0.5 to 1.6
- stoich: float32 [8], replicated, may hold values from -1 to 1
- basis: bfloat16 [96, 8, 256, 32, 128], P(None, None, 'sim', 'learn'), may hold values from -0.006214806 to 0.006214806
- gram_old: float32 [96, 96], replicated, may hold values from -6 to 6
Outputs:
- final_fields: float32 [8, 256, 32, 128], P(None, 'sim', 'learn')
- reduced: float32 [96, 8], replicated
- pod_gram: float32 [96, 96], replicated
- rhs_block: float32 [4752, 96], P('learn')
All inputs are finite; a program needn't handle non-finite values.
Results may differ from a plain program's by a relative error of at most 0.0077.
Values sent between devices are 32-bit elements; how exact they have to be, the bound alone decides.
A program may use at most 64 MiB of HBM per device.

v0:
```python
import functools

import jax
import jax.numpy as jnp
import numpy as np
from jax import lax
from jax.experimental import pallas as pl
from jax.experimental.pallas import tpu as pltpu
from jax.sharding import PartitionSpec as P

MESH = pl.DeviceIdType.MESH
STEPS = 8
PER = 1
W = 2 * PER
NF = 8
CX = 8
CY = 8
XB = CX + 2 * W
YB = CY + 2 * W
MODES = 96
F32 = jnp.float32
BF16 = jnp.bfloat16

time_step = 0.1
drift_x = 1.2
drift_y = 1.0
drift_z = 0.3
arrhenius = 2.0
activation = 1.0

DIRS = [(dx, dy) for dx in (-1, 0, 1) for dy in (-1, 0, 1) if (dx, dy) != (0, 0)]


def face_range(d):
    if d < 0:
        return W, W + CX, W
    if d > 0:
        return CX, 0, W
    return W, W, CX


def pieces():
    out = []
    for dx, dy in DIRS:
        if dx == 0 or dy == 0:
            sx, tx, nx = face_range(dx)
            sy, ty, ny = face_range(dy)
            out.append((dx, dy, sx, sy, tx, ty, nx, ny))
            continue
        for i in range(1, W):
            n = W - i
            sx, tx = (W + i - 1, W + CX + i - 1) if dx < 0 else (W + CX - i, W - i)
            sy, ty = (W, W + CY) if dy < 0 else (W + CY - n, W - n)
            out.append((dx, dy, sx, sy, tx, ty, 1, n))
    return out


PIECES = pieces()


def steps_kernel(
    dims,
    diff_ref,
    stoich_ref,
    fields_ref,
    basis_ref,
    final_ref,
    red_ref,
    state,
    mid,
    rate,
    snaps,
    basis,
    acc,
    part,
    slots_a,
    slots_b,
    basis_sem,
    send_sem,
    recv_sem,
    send_a,
    recv_a,
    send_b,
    recv_b,
):
    (yh_n, z_n, x_n), (yl_n, core_n) = dims
    sims, learns = yh_n * z_n * x_n, yl_n * core_n
    s = lax.axis_index("sim")
    l = lax.axis_index("learn")

    fetch = pltpu.make_async_copy(basis_ref, basis, basis_sem)
    fetch.start()

    state[...] = jnp.zeros_like(state)
    mid[...] = jnp.zeros_like(mid)

    x_me = s % x_n
    z_me = (s // x_n) % z_n
    yh_me = s // (x_n * z_n)
    core_me = l % core_n
    yl_me = l // core_n

    peers_a = []
    na = x_n * core_n
    rank_a = x_me * core_n + core_me
    for k in range(1, na):
        r = (rank_a + k) % na
        peers_a.append(((s - x_me) + r // core_n, (l - core_me) + r % core_n))
    peers_b = []
    nb = yh_n * z_n * yl_n
    rank_b = (yh_me * z_n + z_me) * yl_n + yl_me
    for k in range(1, nb):
        r = (rank_b + k) % nb
        yz = r // yl_n
        peers_b.append((yz * x_n + x_me, (r % yl_n) * core_n + core_me))

    def there(dx, dy):
        ok = None
        for d, me, n in ((dx, s, sims), (dy, l, learns)):
            if d == 0:
                continue
            c = me > 0 if d < 0 else me < n - 1
            ok = c if ok is None else ok & c
        return ok

    barrier = pltpu.get_barrier_semaphore()
    count = jnp.int32(len(peers_a) + len(peers_b))
    for dx, dy in DIRS:
        ok = there(dx, dy)
        count = count + ok.astype(jnp.int32)

        @pl.when(ok)
        def _(dx=dx, dy=dy):
            pl.semaphore_signal(
                barrier, inc=1, device_id={"sim": s + dx, "learn": l + dy}, device_id_type=MESH
            )

    for ps, pl_ in peers_a + peers_b:
        pl.semaphore_signal(barrier, inc=1, device_id={"sim": ps, "learn": pl_}, device_id_type=MESH)

    for f in range(NF):
        for x in range(CX):
            state[W + x, pl.ds(W * 8 + f, 8, stride=8), :] = fields_ref[f * CX + x]

    row = lax.broadcasted_iota(jnp.int32, (8, 128), 0)
    lane = lax.broadcasted_iota(jnp.int32, (8, 128), 1)
    diff = jnp.zeros((8, 128), F32)
    sto = jnp.zeros((8, 128), F32)
    for f in range(NF):
        diff = jnp.where(row == f, diff_ref[f], diff)
        sto = jnp.where(row == f, stoich_ref[f], sto)

    def coefs(scale, keep):
        upper = jnp.where(lane < 127, scale * (diff - 0.5 * drift_z), 0.0)
        lower = jnp.where(lane > 0, scale * (diff + 0.5 * drift_z), 0.0)
        return (
            keep - (6.0 * scale) * diff,
            scale * (diff - 0.5 * drift_x),
            scale * (diff + 0.5 * drift_x),
            scale * (diff - 0.5 * drift_y),
            scale * (diff + 0.5 * drift_y),
            upper,
            lower,
            (scale * arrhenius) * sto,
        )

    coefs_1 = coefs(time_step, 1.0)
    coefs_2 = coefs(0.5 * time_step, 0.5)

    y_low = jnp.where(l > 0, 1.0, 0.0).astype(F32)
    y_high = jnp.where(l < learns - 1, 1.0, 0.0).astype(F32)

    def rates(src, base, r):
        starts = sorted({W - r + 8 * i for i in range((CY + 2 * r) // 8)} | {W + r})
        for x in range(W - r, W + CX + r):
            for y in starts:
                u0 = src[base + x, pl.ds(y * 8, 8, stride=8), :]
                u1 = src[base + x, pl.ds(y * 8 + 1, 8, stride=8), :]
                u7 = src[base + x, pl.ds(y * 8 + 7, 8, stride=8), :]
                rate[x, pl.ds(y, 8), :] = (
                    jnp.tanh(u0) * jnp.tanh(u1) * jnp.exp(-activation / (1.0 + u7 * u7))
                )

    def stage(src, base, dst, dbase, r, cs, old=None, obase=0):
        c_c, c_e, c_w, c_n, c_s, c_u, c_l, c_r = cs
        rates(src, base, r)
        lo = jnp.where(s > 0, W - r, W)
        hi = jnp.where(s < sims - 1, W + CX + r, W + CX)

        def line(x, _):
            cells = {y: src[base + x, pl.ds(y * 8, 8), :] for y in range(W - r - 1, W + CY + r + 1)}
            for y in range(W - r, W + CY + r):
                c = cells[y]
                east = src[base + x + 1, pl.ds(y * 8, 8), :]
                west = src[base + x - 1, pl.ds(y * 8, 8), :]
                q = jnp.broadcast_to(rate[x, pl.ds(y, 1), :], (8, 128))
                v = (c_c * c + c_e * east) + (c_w * west + c_n * cells[y + 1])
                v2 = (c_s * cells[y - 1] + c_r * q) + (
                    c_u * pltpu.roll(c, 127, 1) + c_l * pltpu.roll(c, 1, 1)
                )
                v = v + v2
                if old is not None:
                    v = v + 0.5 * old[obase + x, pl.ds(y * 8, 8), :]
                if y < W:
                    v = v * y_low
                if y >= W + CY:
                    v = v * y_high
                dst[dbase + x, pl.ds(y * 8, 8), :] = v
            return 0

        lax.fori_loop(lo, hi, line, 0)

    def snapshot(base, t):
        for fp in range(NF // 2):
            for xp in range(CX // 2):
                halves = []
                for f in (2 * fp, 2 * fp + 1):
                    a = state[base + W + 2 * xp, pl.ds(W * 8 + f, 8, stride=8), :]
                    b = state[base + W + 2 * xp + 1, pl.ds(W * 8 + f, 8, stride=8), :]
                    halves.append(jnp.concatenate([a, b], axis=0))
                tile = jnp.concatenate(halves, axis=1).astype(BF16)
                snaps[fp * 4 + xp, pl.ds(pl.multiple_of(t * 16, 16), 16), :] = tile

    def copy(par, k):
        dx, dy, sx, sy, tx, ty, nx, ny = PIECES[k]
        return pltpu.make_async_remote_copy(
            src_ref=state.at[pl.ds(par * XB + sx, nx), pl.ds(sy * 8, ny * 8), :],
            dst_ref=state.at[pl.ds(par * XB + tx, nx), pl.ds(ty * 8, ny * 8), :],
            send_sem=send_sem.at[par, k],
            recv_sem=recv_sem.at[par, k],
            device_id={"sim": s + dx, "learn": l + dy},
            device_id_type=MESH,
        )

    pl.semaphore_wait(barrier, count)

    def window(e, _):
        par = lax.rem(e, 2)
        base = par * XB
        nxt = (1 - par) * XB
        for k, p in enumerate(PIECES):

            @pl.when(there(p[0], p[1]))
            def _(k=k):
                copy(par, k).start()

        for k, p in enumerate(PIECES):

            @pl.when(there(-p[0], -p[1]))
            def _(k=k):
                copy(par, k).wait_recv()

        stage(state, base, mid, 0, 1, coefs_1)
        stage(mid, 0, state, nxt, 0, coefs_2, state, base)
        snapshot(nxt, e)
        for k, p in enumerate(PIECES):

            @pl.when(there(p[0], p[1]))
            def _(k=k):
                copy(par, k).wait_send()

        return 0

    lax.fori_loop(0, STEPS, window, 0)

    fetch.wait()
    acc[...] = jnp.zeros_like(acc)

    def block(kb, _):
        fp = kb // 4
        xp = kb % 4
        r0 = pl.multiple_of(fp * 128 + xp * 16, 16)
        lhs = jnp.concatenate(
            [
                basis[:, pl.ds(r0, 16), :].reshape(MODES * 16, 128),
                basis[:, pl.ds(r0 + 64, 16), :].reshape(MODES * 16, 128),
            ],
            axis=1,
        )
        acc[...] += lax.dot_general(
            lhs, snaps[kb], (((1,), (1,)), ((), ())), preferred_element_type=F32
        )
        return 0

    lax.fori_loop(0, 16, block, 0)

    last = (STEPS % 2) * XB
    for f in range(NF):
        for x in range(CX):
            final_ref[f * CX + x] = state[last + W + x, pl.ds(W * 8 + f, 8, stride=8), :]

    r16 = lax.broadcasted_iota(jnp.int32, (16, 128), 0)
    c16 = lax.broadcasted_iota(jnp.int32, (16, 128), 1)
    diagonal = (c16 % 16 == r16).astype(F32)
    kept = jnp.sum(acc[...].reshape(MODES, 16, 128) * diagonal[None], axis=1)
    kept = jnp.concatenate([kept, jnp.zeros((128 - MODES, 128), F32)], axis=0)
    groups = (lane // 16 == row).astype(F32)
    mine = lax.dot_general(
        groups,
        kept,
        (((1,), (1,)), ((), ())),
        precision=lax.Precision.HIGHEST,
        preferred_element_type=F32,
    )

    def share(slots, peers, rank, n, phase, send, recv):
        copies = []
        for k, (ps, pl_) in enumerate(peers):
            c = pltpu.make_async_remote_copy(
                src_ref=part.at[phase],
                dst_ref=slots.at[k],
                send_sem=send.at[k],
                recv_sem=recv.at[k],
                device_id={"sim": ps, "learn": pl_},
                device_id_type=MESH,
            )
            c.start()
            copies.append(c)
        for c in copies:
            c.wait()

    def total(slots, rank, n, phase):
        out = jnp.zeros((8, 128), F32)
        for r in range(n):
            k = lax.rem(rank - r + n - 1 + n, n)
            mine_now = part[phase]
            other = slots[jnp.minimum(k, n - 2)]
            out = out + jnp.where(rank == r, mine_now, other)
        return out

    part[0] = mine
    share(slots_a, peers_a, rank_a, na, 0, send_a, recv_a)
    part[1] = total(slots_a, rank_a, na, 0)
    share(slots_b, peers_b, rank_b, nb, 1, send_b, recv_b)
    red_ref[...] = total(slots_b, rank_b, nb, 1)


def split3(v):
    hi = v.astype(BF16).astype(F32)
    rest = v - hi
    mi = rest.astype(BF16).astype(F32)
    return hi, mi, rest - mi


def outer_sum(a, b):
    ah, am, al = split3(a)
    bh, bm, bl = split3(b)
    left = jnp.concatenate([ah, ah, am, am, ah, al], axis=0).astype(BF16)
    right = jnp.concatenate([bh, bm, bh, bm, bl, bh], axis=0).astype(BF16)
    return lax.dot_general(left, right, (((0,), (0,)), ((), ())), preferred_element_type=F32)


def tail_kernel(rows, red_ref, gram_ref, first_ref, second_ref, reduced_ref, pod_ref, rhs_ref):
    l = lax.axis_index("learn")
    red = red_ref[...]
    row = lax.broadcasted_iota(jnp.int32, (8, 128), 0)
    lane = lax.broadcasted_iota(jnp.int32, (8, 128), 1)
    reduced_ref[...] = red.T[:MODES]
    pod_ref[...] = gram_ref[...] + outer_sum(red, red)[:MODES, :MODES]
    widened = jnp.where(lane == 0, 1.0, pltpu.roll(red, 1, 1))
    changes = jnp.where(row < STEPS - 1, pltpu.roll(red, 7, 0) - red, 0.0)
    feats = []
    for j in range(first_ref.shape[1]):
        one = jnp.broadcast_to(first_ref[l, pl.ds(j, 1), :], (8, 128))
        two = jnp.broadcast_to(second_ref[l, pl.ds(j, 1), :], (8, 128))
        feats.append(
            jnp.take_along_axis(widened, one, axis=1, mode="promise_in_bounds")
            * jnp.take_along_axis(widened, two, axis=1, mode="promise_in_bounds")
        )
    feats = jnp.concatenate(feats, axis=1)
    rhs_ref[...] = outer_sum(feats, changes)[:rows, :MODES]


def pair_tables(modes, blocks):
    upper_pairs = np.triu_indices(modes)
    first = np.concatenate([np.zeros(modes), upper_pairs[0] + 1]).astype(np.int32)
    second = np.concatenate([np.arange(modes) + 1, upper_pairs[1] + 1]).astype(np.int32)
    rows = first.shape[0] // blocks
    lines = -(-rows // 128)

    def lay(t):
        t = t.reshape(blocks, rows)
        t = np.pad(t, ((0, 0), (0, lines * 128 - rows)))
        return t.reshape(blocks, lines, 128)

    return rows, lay(first), lay(second)


def solution(mesh):
    sims, learns = mesh.shape["sim"], mesh.shape["learn"]
    dims = ((2, 4, 4), (2, 2)) if (sims, learns) == (32, 4) else ((1, 1, sims), (1, learns))
    (yh_n, z_n, x_n), (yl_n, core_n) = dims
    na, nb = x_n * core_n, yh_n * z_n * yl_n
    rows, first, second = pair_tables(MODES, learns)
    vmem = pl.BlockSpec(memory_space=pltpu.VMEM)
    smem = pl.BlockSpec(memory_space=pltpu.SMEM)
    n_pieces = len(PIECES)

    def body(fields, diffusivity, stoich, basis, gram_old):
        flat = basis.reshape(MODES, NF * CX * CY, 128)
        final, red = pl.pallas_call(
            functools.partial(steps_kernel, dims),
            out_shape=(
                jax.ShapeDtypeStruct((NF * CX, CY, 128), F32),
                jax.ShapeDtypeStruct((8, 128), F32),
            ),
            in_specs=[smem, smem, vmem, pl.BlockSpec(memory_space=pl.ANY)],
            out_specs=(vmem, vmem),
            scratch_shapes=[
                pltpu.VMEM((2 * XB, YB * 8, 128), F32),
                pltpu.VMEM((XB, YB * 8, 128), F32),
                pltpu.VMEM((XB, -(-YB // 8) * 8, 128), F32),
                pltpu.VMEM((16, 128, 256), BF16),
                pltpu.VMEM((MODES, NF * CX * CY, 128), BF16),
                pltpu.VMEM((MODES * 16, 128), F32),
                pltpu.VMEM((2, 8, 128), F32),
                pltpu.VMEM((max(na - 1, 1), 8, 128), F32),
                pltpu.VMEM((max(nb - 1, 1), 8, 128), F32),
                pltpu.SemaphoreType.DMA,
                pltpu.SemaphoreType.DMA((2, n_pieces)),
                pltpu.SemaphoreType.DMA((2, n_pieces)),
                pltpu.SemaphoreType.DMA((max(na - 1, 1),)),
                pltpu.SemaphoreType.DMA((max(na - 1, 1),)),
                pltpu.SemaphoreType.DMA((max(nb - 1, 1),)),
                pltpu.SemaphoreType.DMA((max(nb - 1, 1),)),
            ],
            compiler_params=pltpu.CompilerParams(
                collective_id=0, has_side_effects=True, vmem_limit_bytes=44 * 1024 * 1024
            ),
            name="steps",
        )(diffusivity, stoich, fields.reshape(NF * CX, CY, 128), flat)
        reduced, pod, rhs = pl.pallas_call(
            functools.partial(tail_kernel, rows),
            out_shape=(
                jax.ShapeDtypeStruct((MODES, STEPS), F32),
                jax.ShapeDtypeStruct((MODES, MODES), F32),
                jax.ShapeDtypeStruct((rows, MODES), F32),
            ),
            in_specs=[vmem] * 4,
            out_specs=(vmem,) * 3,
            name="tail",
        )(red, gram_old, jnp.asarray(first), jnp.asarray(second))
        return final.reshape(NF, CX, CY, 128), reduced, pod, rhs

    in_specs = (
        P(None, "sim", "learn", None),
        P(),
        P(),
        P(None, None, "sim", "learn", None),
        P(),
    )
    out_specs = (P(None, "sim", "learn", None), P(), P(), P("learn", None))
    return jax.shard_map(body, mesh=mesh, in_specs=in_specs, out_specs=out_specs, check_vma=False)
```

profile of v0, /device:TPU:1, one launch (start us, length us, event | category | flops | bytes accessed | tf_op | source)
XLA Modules:
  0.0 97.9 jit_solution(10985113308526090420)
XLA Ops:
  0.6 0.0 copy-start
  0.6 0.9 copy-done
  1.6 0.0 copy-start.2
  1.6 0.7 copy-done.2
  2.2 0.0 copy-start.3
  2.2 0.7 copy-done.3
  2.9 88.1 %steps.1 = (f32[64,8,128]{2,1,0:T(8,128)S(1)}, f32[8,128]{1,0:T(8,128)S(1)}) custom-call(f32[8]{0:T(128)S(1)} %copy-done.2, f32[8]{0:T(128)S(1)} %copy-done.3, f32[64,8,128]{2,1,0:T(8,128)S(1)} %bitcast.3, bf16[96,512,128]{2,1,0:T(8,128)(2,1)} %bitcast.5), custom_call_target="tpu_custom_call" | custom-call | tf_op jit(solution)/shard_map/steps/pallas_call | solution.py:401
  91.0 0.0 copy-start.1
  91.0 0.6 copy-done.1
  91.5 2.1 %tail.1 = (f32[96,8]{1,0:T(8,128)}, f32[96,96]{1,0:T(8,128)}, f32[1188,96]{1,0:T(8,128)}) custom-call(f32[8,128]{1,0:T(8,128)} %copy-done.1, f32[96,96]{1,0:T(8,128)} %gram_ref.1, s32[4,10,128]{2,1,0:T(8,128)} %constant.4.clone.first_ref, s32[4,10,128]{2,1,0:T(8,128)} %constant.5.clone.second_ref), custom_call_target="tpu_custom_call" | custom-call | tf_op jit(solution)/shard_map/tail/pallas_call | solution.py:432
  93.7 1.5 %copy.11 = f32[96,8]{0,1:T(8,128)} copy(f32[96,8]{1,0:T(8,128)} %get-tuple-element.15) | data formatting | bytes 6144
  95.1 2.1 %copy.12 = f32[1188,96]{0,1:T(8,128)} copy(f32[1188,96]{1,0:T(8,128)} %get-tuple-element.17) | data formatting | bytes 912384
  97.2 0.7 copy.14
Async XLA Ops:
  0.6 1.0 copy-start
  1.6 0.7 copy-start.2
  2.2 0.7 copy-start.3
  91.0 0.6 copy-start.1
where the time goes:
time: 98.2 us; the launch traced here: 97.9 us
  Pallas kernels  90.2 us (92%)
  local copies, waits for them, and re-layouts  7.08 us (7%)
    pallas_call x1, Pallas kernels, body(): pl.pallas_call(functools.partial(steps_kernel, dims), out_shape=(jax.Shap...  88.1 us
    unnamed x11, local copies, waits for them, and re-layouts  7.08 us
    pallas_call x1, Pallas kernels, body(): pl.pallas_call(functools.partial(tail_kernel, rows), out_shape=(jax.Shape...  2.11 us

commit v1 on v0

--- a/solution.py
+++ b/solution.py
@@ -10,7 +10,7 @@
 
 MESH = pl.DeviceIdType.MESH
 STEPS = 8
-PER = 1
+PER = 4
 W = 2 * PER
 NF = 8
 CX = 8
@@ -28,7 +28,9 @@
 arrhenius = 2.0
 activation = 1.0
 
-DIRS = [(dx, dy) for dx in (-1, 0, 1) for dy in (-1, 0, 1) if (dx, dy) != (0, 0)]
+SIDES = ((-1, 0), (1, 0), (0, -1), (0, 1))
+
+CORNERS = {2: ((1, 1, 1),), 4: ((1, 3, 3),), 6: ((1, 5, 5),), 8: ((1, 4, 7), (5, 7, 3))}[W]
 
 
 def face_range(d):
@@ -41,17 +43,16 @@
 
 def pieces():
     out = []
-    for dx, dy in DIRS:
-        if dx == 0 or dy == 0:
-            sx, tx, nx = face_range(dx)
-            sy, ty, ny = face_range(dy)
-            out.append((dx, dy, sx, sy, tx, ty, nx, ny))
-            continue
-        for i in range(1, W):
-            n = W - i
-            sx, tx = (W + i - 1, W + CX + i - 1) if dx < 0 else (W + CX - i, W - i)
-            sy, ty = (W, W + CY) if dy < 0 else (W + CY - n, W - n)
-            out.append((dx, dy, sx, sy, tx, ty, 1, n))
+    for dx, dy in SIDES:
+        sx, tx, nx = face_range(dx)
+        sy, ty, ny = face_range(dy)
+        out.append((dx, dy, 0, sx, sy, tx, ty, nx, ny))
+    for side in (-1, 1):
+        for dy in (-1, 1):
+            for i0, i1, n in CORNERS:
+                x = W - i1 if side < 0 else W + CX + i0 - 1
+                sy, ty = (W, W + CY) if dy < 0 else (W + CY - n, W - n)
+                out.append((0, dy, side, x, sy, x, ty, i1 - i0 + 1, n))
     return out
 
 
@@ -60,18 +61,23 @@
 
 def steps_kernel(
     dims,
-    diff_ref,
-    stoich_ref,
-    fields_ref,
+    diff_hbm,
+    stoich_hbm,
+    fields_hbm,
     basis_ref,
     final_ref,
     red_ref,
     state,
     mid,
+    later,
     rate,
     snaps,
     basis,
     acc,
+    diff_ref,
+    stoich_ref,
+    fields_ref,
+    in_sem,
     part,
     slots_a,
     slots_b,
@@ -89,10 +95,28 @@
     l = lax.axis_index("learn")
 
     fetch = pltpu.make_async_copy(basis_ref, basis, basis_sem)
+    loads = [
+        pltpu.make_async_copy(a, b, in_sem.at[i])
+        for i, (a, b) in enumerate(
+            ((fields_hbm, fields_ref), (diff_hbm, diff_ref), (stoich_hbm, stoich_ref))
+        )
+    ]
+    for c in loads:
+        c.start()
     fetch.start()
 
-    state[...] = jnp.zeros_like(state)
-    mid[...] = jnp.zeros_like(mid)
+    for par in range(2):
+        for edge, x in ((s == 0, par * XB), (s == lax.axis_size("sim") - 1, par * XB + W + CX)):
+
+            @pl.when(edge)
+            def _(x=x):
+                state[pl.ds(x, W)] = jnp.zeros((W, YB * 8, 128), F32)
+
+        for edge, y in ((l == 0, 0), (l == lax.axis_size("learn") - 1, W + CY)):
+
+            @pl.when(edge)
+            def _(par=par, y=y):
+                state[pl.ds(par * XB, XB), pl.ds(y * 8, W * 8), :] = jnp.zeros((XB, W * 8, 128), F32)
 
     x_me = s % x_n
     z_me = (s // x_n) % z_n
@@ -125,7 +149,7 @@
 
     barrier = pltpu.get_barrier_semaphore()
     count = jnp.int32(len(peers_a) + len(peers_b))
-    for dx, dy in DIRS:
+    for dx, dy in SIDES:
         ok = there(dx, dy)
         count = count + ok.astype(jnp.int32)
 
@@ -137,6 +161,9 @@
 
     for ps, pl_ in peers_a + peers_b:
         pl.semaphore_signal(barrier, inc=1, device_id={"sim": ps, "learn": pl_}, device_id_type=MESH)
+
+    for c in loads:
+        c.wait()
 
     for f in range(NF):
         for x in range(CX):
@@ -167,13 +194,19 @@
     coefs_1 = coefs(time_step, 1.0)
     coefs_2 = coefs(0.5 * time_step, 0.5)
 
+    x_low = jnp.where(s > 0, 1.0, 0.0).astype(F32)
+    x_high = jnp.where(s < sims - 1, 1.0, 0.0).astype(F32)
     y_low = jnp.where(l > 0, 1.0, 0.0).astype(F32)
     y_high = jnp.where(l < learns - 1, 1.0, 0.0).astype(F32)
 
+    def lines(r):
+        for x in range(W - r, W + CX + r):
+            beyond = max(W - x, x - (W + CX - 1), 0)
+            yield x, W - (r - beyond), W + CY + (r - beyond)
+
     def rates(src, base, r):
-        starts = sorted({W - r + 8 * i for i in range((CY + 2 * r) // 8)} | {W + r})
-        for x in range(W - r, W + CX + r):
-            for y in starts:
+        for x, y0, y1 in lines(r):
+            for y in sorted({min(y, y1 - 8) for y in range(y0, y1, 8)}):
                 u0 = src[base + x, pl.ds(y * 8, 8, stride=8), :]
                 u1 = src[base + x, pl.ds(y * 8 + 1, 8, stride=8), :]
                 u7 = src[base + x, pl.ds(y * 8 + 7, 8, stride=8), :]
@@ -182,47 +215,52 @@
                 )
 
     def stage(src, base, dst, dbase, r, cs, old=None, obase=0):
-        c_c, c_e, c_w, c_n, c_s, c_u, c_l, c_r = cs
+        c_c, c_e, c_w, c_n, c_s, c_u, c_l, c_r = (c[None] for c in cs)
         rates(src, base, r)
-        lo = jnp.where(s > 0, W - r, W)
-        hi = jnp.where(s < sims - 1, W + CX + r, W + CX)
-
-        def line(x, _):
-            cells = {y: src[base + x, pl.ds(y * 8, 8), :] for y in range(W - r - 1, W + CY + r + 1)}
-            for y in range(W - r, W + CY + r):
-                c = cells[y]
-                east = src[base + x + 1, pl.ds(y * 8, 8), :]
-                west = src[base + x - 1, pl.ds(y * 8, 8), :]
-                q = jnp.broadcast_to(rate[x, pl.ds(y, 1), :], (8, 128))
-                v = (c_c * c + c_e * east) + (c_w * west + c_n * cells[y + 1])
-                v2 = (c_s * cells[y - 1] + c_r * q) + (
-                    c_u * pltpu.roll(c, 127, 1) + c_l * pltpu.roll(c, 1, 1)
+
+        def cells(ref, x, y, n):
+            return ref[x, pl.ds(y * 8, n * 8), :].reshape(n, 8, 128)
+
+        for x, y0, y1 in lines(r):
+            cuts = sorted({y0, y1} | {y for y in (W, W + CY) if y0 < y < y1})
+            for y, end in zip(cuts[:-1], cuts[1:]):
+                n = end - y
+                c = cells(src, base + x, y, n)
+                q = jnp.stack(
+                    [jnp.broadcast_to(rate[x, pl.ds(y + j, 1), :], (8, 128)) for j in range(n)]
                 )
-                v = v + v2
+                v = c_c * c + c_e * cells(src, base + x + 1, y, n)
+                v = v + (c_w * cells(src, base + x - 1, y, n) + c_n * cells(src, base + x, y + 1, n))
+                v = v + (c_s * cells(src, base + x, y - 1, n) + c_r * q)
+                v = v + (c_u * pltpu.roll(c, 127, 2) + c_l * pltpu.roll(c, 1, 2))
                 if old is not None:
-                    v = v + 0.5 * old[obase + x, pl.ds(y * 8, 8), :]
+                    v = v + 0.5 * cells(old, obase + x, y, n)
+                masks = []
+                if x < W:
+                    masks.append(x_low)
+                if x >= W + CX:
+                    masks.append(x_high)
                 if y < W:
-                    v = v * y_low
+                    masks.append(y_low)
                 if y >= W + CY:
-                    v = v * y_high
-                dst[dbase + x, pl.ds(y * 8, 8), :] = v
-            return 0
-
-        lax.fori_loop(lo, hi, line, 0)
-
-    def snapshot(base, t):
+                    masks.append(y_high)
+                if masks:
+                    v = v * functools.reduce(lambda a, b: a * b, masks)
+                dst[dbase + x, pl.ds(y * 8, n * 8), :] = v.reshape(n * 8, 128)
+
+    def snapshot(src, base, t):
         for fp in range(NF // 2):
             for xp in range(CX // 2):
                 halves = []
                 for f in (2 * fp, 2 * fp + 1):
-                    a = state[base + W + 2 * xp, pl.ds(W * 8 + f, 8, stride=8), :]
-                    b = state[base + W + 2 * xp + 1, pl.ds(W * 8 + f, 8, stride=8), :]
+                    a = src[base + W + 2 * xp, pl.ds(W * 8 + f, 8, stride=8), :]
+                    b = src[base + W + 2 * xp + 1, pl.ds(W * 8 + f, 8, stride=8), :]
                     halves.append(jnp.concatenate([a, b], axis=0))
                 tile = jnp.concatenate(halves, axis=1).astype(BF16)
                 snaps[fp * 4 + xp, pl.ds(pl.multiple_of(t * 16, 16), 16), :] = tile
 
     def copy(par, k):
-        dx, dy, sx, sy, tx, ty, nx, ny = PIECES[k]
+        dx, dy, _, sx, sy, tx, ty, nx, ny = PIECES[k]
         return pltpu.make_async_remote_copy(
             src_ref=state.at[pl.ds(par * XB + sx, nx), pl.ds(sy * 8, ny * 8), :],
             dst_ref=state.at[pl.ds(par * XB + tx, nx), pl.ds(ty * 8, ny * 8), :],
@@ -238,30 +276,39 @@
         par = lax.rem(e, 2)
         base = par * XB
         nxt = (1 - par) * XB
-        for k, p in enumerate(PIECES):
-
-            @pl.when(there(p[0], p[1]))
-            def _(k=k):
-                copy(par, k).start()
-
-        for k, p in enumerate(PIECES):
-
-            @pl.when(there(-p[0], -p[1]))
-            def _(k=k):
-                copy(par, k).wait_recv()
-
-        stage(state, base, mid, 0, 1, coefs_1)
-        stage(mid, 0, state, nxt, 0, coefs_2, state, base)
-        snapshot(nxt, e)
-        for k, p in enumerate(PIECES):
-
-            @pl.when(there(p[0], p[1]))
-            def _(k=k):
-                copy(par, k).wait_send()
-
+
+        def each(chosen, act, arriving):
+            for k in chosen:
+                dx, dy, side = PIECES[k][:3]
+                ok = there(-dx, -dy) if arriving else there(dx, dy)
+                if side:
+                    ok = ok & there(side, 0)
+
+                @pl.when(ok)
+                def _(k=k):
+                    act(copy(par, k))
+
+        every = range(len(PIECES))
+        send = lambda c: c.start()
+        arrive = lambda c: c.wait_recv()
+        each(range(4), send, False)
+        for face, side in ((1, -1), (0, 1)):
+            each([face], arrive, True)
+            each([k for k in every if PIECES[k][2] == side], send, False)
+        each(range(2, len(PIECES)), arrive, True)
+
+        src, sbase = state, base
+        for k in range(PER):
+            r = W - 2 * k
+            stage(src, sbase, mid, 0, r - 1, coefs_1)
+            dst, dbase = (state, nxt) if k == PER - 1 else (later, (k % 2) * XB)
+            stage(mid, 0, dst, dbase, r - 2, coefs_2, src, sbase)
+            snapshot(dst, dbase, e * PER + k)
+            src, sbase = dst, dbase
+        each(every, lambda c: c.wait_send(), False)
         return 0
 
-    lax.fori_loop(0, STEPS, window, 0)
+    lax.fori_loop(0, STEPS // PER, window, 0)
 
     fetch.wait()
     acc[...] = jnp.zeros_like(acc)
@@ -284,7 +331,7 @@
 
     lax.fori_loop(0, 16, block, 0)
 
-    last = (STEPS % 2) * XB
+    last = (STEPS // PER % 2) * XB
     for f in range(NF):
         for x in range(CX):
             final_ref[f * CX + x] = state[last + W + x, pl.ds(W * 8 + f, 8, stride=8), :]
@@ -350,12 +397,16 @@
     return lax.dot_general(left, right, (((0,), (0,)), ((), ())), preferred_element_type=F32)
 
 
-def tail_kernel(rows, red_ref, gram_ref, first_ref, second_ref, reduced_ref, pod_ref, rhs_ref):
+def tail_kernel(
+    rows, red_ref, gram_ref, first_ref, second_ref, state_ref, reduced_ref, pod_ref, rhs_ref, final_ref, sem
+):
+    keep = pltpu.make_async_copy(state_ref, final_ref, sem)
+    keep.start()
     l = lax.axis_index("learn")
     red = red_ref[...]
     row = lax.broadcasted_iota(jnp.int32, (8, 128), 0)
     lane = lax.broadcasted_iota(jnp.int32, (8, 128), 1)
-    reduced_ref[...] = red.T[:MODES]
+    reduced_ref[...] = red[:, :MODES]
     pod_ref[...] = gram_ref[...] + outer_sum(red, red)[:MODES, :MODES]
     widened = jnp.where(lane == 0, 1.0, pltpu.roll(red, 1, 1))
     changes = jnp.where(row < STEPS - 1, pltpu.roll(red, 7, 0) - red, 0.0)
@@ -368,7 +419,8 @@
             * jnp.take_along_axis(widened, two, axis=1, mode="promise_in_bounds")
         )
     feats = jnp.concatenate(feats, axis=1)
-    rhs_ref[...] = outer_sum(feats, changes)[:rows, :MODES]
+    rhs_ref[...] = outer_sum(changes, feats)[:MODES, :rows]
+    keep.wait()
 
 
 def pair_tables(modes, blocks):
@@ -393,7 +445,7 @@
     na, nb = x_n * core_n, yh_n * z_n * yl_n
     rows, first, second = pair_tables(MODES, learns)
     vmem = pl.BlockSpec(memory_space=pltpu.VMEM)
-    smem = pl.BlockSpec(memory_space=pltpu.SMEM)
+    hbm = pl.BlockSpec(memory_space=pl.ANY)
     n_pieces = len(PIECES)
 
     def body(fields, diffusivity, stoich, basis, gram_old):
@@ -404,15 +456,20 @@
                 jax.ShapeDtypeStruct((NF * CX, CY, 128), F32),
                 jax.ShapeDtypeStruct((8, 128), F32),
             ),
-            in_specs=[smem, smem, vmem, pl.BlockSpec(memory_space=pl.ANY)],
+            in_specs=[hbm] * 4,
             out_specs=(vmem, vmem),
             scratch_shapes=[
                 pltpu.VMEM((2 * XB, YB * 8, 128), F32),
                 pltpu.VMEM((XB, YB * 8, 128), F32),
+                pltpu.VMEM((2 * XB, YB * 8, 128), F32),
                 pltpu.VMEM((XB, -(-YB // 8) * 8, 128), F32),
                 pltpu.VMEM((16, 128, 256), BF16),
                 pltpu.VMEM((MODES, NF * CX * CY, 128), BF16),
                 pltpu.VMEM((MODES * 16, 128), F32),
+                pltpu.SMEM((NF,), F32),
+                pltpu.SMEM((NF,), F32),
+                pltpu.VMEM((NF * CX, CY, 128), F32),
+                pltpu.SemaphoreType.DMA((3,)),
                 pltpu.VMEM((2, 8, 128), F32),
                 pltpu.VMEM((max(na - 1, 1), 8, 128), F32),
                 pltpu.VMEM((max(nb - 1, 1), 8, 128), F32),
@@ -425,22 +482,25 @@
                 pltpu.SemaphoreType.DMA((max(nb - 1, 1),)),
             ],
             compiler_params=pltpu.CompilerParams(
-                collective_id=0, has_side_effects=True, vmem_limit_bytes=44 * 1024 * 1024
+                collective_id=0, has_side_effects=True, vmem_limit_bytes=60 * 1024 * 1024
             ),
             name="steps",
         )(diffusivity, stoich, fields.reshape(NF * CX, CY, 128), flat)
-        reduced, pod, rhs = pl.pallas_call(
+        reduced, pod, rhs, final = pl.pallas_call(
             functools.partial(tail_kernel, rows),
             out_shape=(
-                jax.ShapeDtypeStruct((MODES, STEPS), F32),
+                jax.ShapeDtypeStruct((STEPS, MODES), F32),
                 jax.ShapeDtypeStruct((MODES, MODES), F32),
-                jax.ShapeDtypeStruct((rows, MODES), F32),
+                jax.ShapeDtypeStruct((MODES, rows), F32),
+                jax.ShapeDtypeStruct((NF * CX, CY, 128), F32),
             ),
-            in_specs=[vmem] * 4,
-            out_specs=(vmem,) * 3,
+            in_specs=[vmem] * 4 + [hbm],
+            out_specs=(vmem,) * 3 + (hbm,),
+            scratch_shapes=[pltpu.SemaphoreType.DMA],
+            compiler_params=pltpu.CompilerParams(vmem_limit_bytes=60 * 1024 * 1024),
             name="tail",
-        )(red, gram_old, jnp.asarray(first), jnp.asarray(second))
-        return final.reshape(NF, CX, CY, 128), reduced, pod, rhs
+        )(red, gram_old, jnp.asarray(first), jnp.asarray(second), final)
+        return final.reshape(NF, CX, CY, 128), reduced.T, pod, rhs.T
 
     in_specs = (
         P(None, "sim", "learn", None),

time: 98.2 us -> 70.9 us (0.72)
  Pallas kernels: 90.2 us -> 70.1 us
  local copies, waits for them, and re-layouts: 7.08 us -> 0 us
    pallas_call x1, Pallas kernels: 88.1 us -> 59.5 us  [body(): pl.pallas_call(functools.partial(steps_kernel, dims), out_shape=(jax.Shap...]
    pallas_call x1, Pallas kernels: 2.11 us -> 10.7 us  [body(): pl.pallas_call(functools.partial(tail_kernel, rows), out_shape=(jax.Shape...]
    unnamed x11 -> x0, local copies, waits for them, and re-layouts: 7.08 us -> none
where the time goes in v1:
time: 70.9 us; the launch traced here: 70.8 us
  Pallas kernels  70.1 us (99%)
    pallas_call x1, Pallas kernels, body(): pl.pallas_call(functools.partial(steps_kernel, dims), out_shape=(jax.Shap...  59.5 us
    pallas_call x1, Pallas kernels, body(): pl.pallas_call(functools.partial(tail_kernel, rows), out_shape=(jax.Shape...  10.7 us

profile of v1, /device:TPU:1, one launch (start us, length us, event | category | flops | bytes accessed | tf_op | source)
XLA Modules:
  0.0 70.8 jit_solution(7304450816765462829)
XLA Ops:
  0.6 59.5 %steps.1 = (f32[64,8,128]{2,1,0:T(8,128)}, f32[8,128]{1,0:T(8,128)}) custom-call(f32[8]{0:T(128)} %diff_hbm.1, f32[8]{0:T(128)} %stoich_hbm.1, f32[64,8,128]{2,1,0:T(8,128)} %bitcast.6, bf16[96,512,128]{2,1,0:T(8,128)(2,1)} %bitcast.5), custom_call_target="tpu_custom_call" | custom-call | tf_op jit(solution)/shard_map/steps/pallas_call | solution.py:453
  60.1 10.7 %tail.1 = (f32[8,96]{1,0:T(8,128)}, f32[96,96]{1,0:T(8,128)}, f32[96,1188]{1,0:T(8,128)}, f32[64,8,128]{2,1,0:T(8,128)}) custom-call(f32[8,128]{1,0:T(8,128)} %get-tuple-element.10.red_ref, f32[96,96]{1,0:T(8,128)} %gram_ref.1, s32[4,10,128]{2,1,0:T(8,128)} %constant.4.clone.first_ref, s32[4,10,128]{2,1,0:T(8,128)} %constant.5.clone.second_ref, ...), custom_call_target="tpu_custom_call" | custom-call | tf_op jit(solution)/shard_map/tail/pallas_call | solution.py:489

commit v2 on v1

--- a/solution.py
+++ b/solution.py
@@ -28,35 +28,49 @@
 arrhenius = 2.0
 activation = 1.0
 
-SIDES = ((-1, 0), (1, 0), (0, -1), (0, 1))
-
-CORNERS = {2: ((1, 1, 1),), 4: ((1, 3, 3),), 6: ((1, 5, 5),), 8: ((1, 4, 7), (5, 7, 3))}[W]
-
-
-def face_range(d):
-    if d < 0:
-        return W, W + CX, W
-    if d > 0:
-        return CX, 0, W
-    return W, W, CX
+DIRS = [(dx, dy) for dx in (-1, 0, 1) for dy in (-1, 0, 1) if (dx, dy) != (0, 0)]
+
+GROUPS = ((1, 2), (3, 4), (5, 6), (7, 8))
+NEAR = 2
 
 
 def pieces():
-    out = []
-    for dx, dy in SIDES:
-        sx, tx, nx = face_range(dx)
-        sy, ty, ny = face_range(dy)
-        out.append((dx, dy, 0, sx, sy, tx, ty, nx, ny))
-    for side in (-1, 1):
-        for dy in (-1, 1):
-            for i0, i1, n in CORNERS:
-                x = W - i1 if side < 0 else W + CX + i0 - 1
-                sy, ty = (W, W + CY) if dy < 0 else (W + CY - n, W - n)
-                out.append((0, dy, side, x, sy, x, ty, i1 - i0 + 1, n))
-    return out
-
-
-PIECES = pieces()
+    out, names = [], {}
+
+    def add(name, *piece):
+        names[name] = len(out)
+        out.append(piece)
+
+    def along_y(dy, n):
+        return (W, W + CY) if dy < 0 else (W + CY - n, W - n)
+
+    for g, (a, b) in enumerate(GROUPS):
+        n = b - a + 1
+        for dx in (-1, 1):
+            sx, tx = (W + a - 1, W + CX + a - 1) if dx < 0 else (W + CX - b, W - b)
+            add(("x", g, dx), dx, 0, 0, sx, W, tx, W, n, CY)
+        if g == 0:
+            for dy in (-1, 1):
+                sy, ty = along_y(dy, CY)
+                add(("y", dy), 0, dy, 0, W, sy, W, ty, CX, CY)
+        rows = min(n, W - a)
+        for dx in (-1, 1):
+            sx, tx = (W + a - 1, W + CX + a - 1) if dx < 0 else (W + CX - a - rows + 1, W - a - rows + 1)
+            for dy in (-1, 1):
+                sy, ty = along_y(dy, W - a)
+                add(("d", g, dx, dy), dx, dy, 0, sx, sy, tx, ty, rows, W - a)
+    direct = len(out)
+    for g, (a, b) in enumerate(GROUPS[:NEAR]):
+        for side in (-1, 1):
+            x = W - b if side < 0 else W + CX + a - 1
+            for dy in (-1, 1):
+                sy, ty = along_y(dy, W - a)
+                add(("f", g, side, dy), 0, dy, side, x, sy, x, ty, b - a + 1, W - a)
+    return out, names, direct
+
+
+PIECES, NAMES, DIRECT = pieces()
+FAR = [NAMES["d", g, dx, dy] for g in range(NEAR) for dx in (-1, 1) for dy in (-1, 1)]
 
 
 def steps_kernel(
@@ -147,9 +161,12 @@
             ok = c if ok is None else ok & c
         return ok
 
+    def on_chip(dy, arriving):
+        return core_me == (0 if (dy > 0) != arriving else 1)
+
     barrier = pltpu.get_barrier_semaphore()
     count = jnp.int32(len(peers_a) + len(peers_b))
-    for dx, dy in SIDES:
+    for dx, dy in DIRS:
         ok = there(dx, dy)
         count = count + ok.astype(jnp.int32)
 
@@ -199,54 +216,57 @@
     y_low = jnp.where(l > 0, 1.0, 0.0).astype(F32)
     y_high = jnp.where(l < learns - 1, 1.0, 0.0).astype(F32)
 
-    def lines(r):
-        for x in range(W - r, W + CX + r):
-            beyond = max(W - x, x - (W + CX - 1), 0)
-            yield x, W - (r - beyond), W + CY + (r - beyond)
-
-    def rates(src, base, r):
-        for x, y0, y1 in lines(r):
-            for y in sorted({min(y, y1 - 8) for y in range(y0, y1, 8)}):
-                u0 = src[base + x, pl.ds(y * 8, 8, stride=8), :]
-                u1 = src[base + x, pl.ds(y * 8 + 1, 8, stride=8), :]
-                u7 = src[base + x, pl.ds(y * 8 + 7, 8, stride=8), :]
-                rate[x, pl.ds(y, 8), :] = (
-                    jnp.tanh(u0) * jnp.tanh(u1) * jnp.exp(-activation / (1.0 + u7 * u7))
-                )
-
-    def stage(src, base, dst, dbase, r, cs, old=None, obase=0):
+    def beyond(x):
+        return max(W - x, x - (W + CX - 1))
+
+    def reach(s_, x):
+        e = W - s_ - max(beyond(x), 0)
+        return W - e, W + CY + e
+
+    def rates(s_, src, base, x):
+        y0, y1 = reach(s_, x)
+        for y in sorted({min(y, y1 - 8) for y in range(y0, y1, 8)}):
+            u0 = src[base + x, pl.ds(y * 8, 8, stride=8), :]
+            u1 = src[base + x, pl.ds(y * 8 + 1, 8, stride=8), :]
+            u7 = src[base + x, pl.ds(y * 8 + 7, 8, stride=8), :]
+            rate[(s_ - 1) * XB + x, pl.ds(y, 8), :] = (
+                jnp.tanh(u0) * jnp.tanh(u1) * jnp.exp(-activation / (1.0 + u7 * u7))
+            )
+
+    def cells(ref, x, y, n):
+        return ref[x, pl.ds(y * 8, n * 8), :].reshape(n, 8, 128)
+
+    def line(s_, src, base, dst, dbase, x, cs, old=None, obase=0):
         c_c, c_e, c_w, c_n, c_s, c_u, c_l, c_r = (c[None] for c in cs)
-        rates(src, base, r)
-
-        def cells(ref, x, y, n):
-            return ref[x, pl.ds(y * 8, n * 8), :].reshape(n, 8, 128)
-
-        for x, y0, y1 in lines(r):
-            cuts = sorted({y0, y1} | {y for y in (W, W + CY) if y0 < y < y1})
-            for y, end in zip(cuts[:-1], cuts[1:]):
-                n = end - y
-                c = cells(src, base + x, y, n)
-                q = jnp.stack(
-                    [jnp.broadcast_to(rate[x, pl.ds(y + j, 1), :], (8, 128)) for j in range(n)]
-                )
-                v = c_c * c + c_e * cells(src, base + x + 1, y, n)
-                v = v + (c_w * cells(src, base + x - 1, y, n) + c_n * cells(src, base + x, y + 1, n))
-                v = v + (c_s * cells(src, base + x, y - 1, n) + c_r * q)
-                v = v + (c_u * pltpu.roll(c, 127, 2) + c_l * pltpu.roll(c, 1, 2))
-                if old is not None:
-                    v = v + 0.5 * cells(old, obase + x, y, n)
-                masks = []
-                if x < W:
-                    masks.append(x_low)
-                if x >= W + CX:
-                    masks.append(x_high)
-                if y < W:
-                    masks.append(y_low)
-                if y >= W + CY:
-                    masks.append(y_high)
-                if masks:
-                    v = v * functools.reduce(lambda a, b: a * b, masks)
-                dst[dbase + x, pl.ds(y * 8, n * 8), :] = v.reshape(n * 8, 128)
+        y0, y1 = reach(s_, x)
+        ends = sorted({y0, y1} | {y for y in (W, W + CY) if y0 < y < y1})
+        for y, end in zip(ends[:-1], ends[1:]):
+            n = end - y
+            c = cells(src, base + x, y, n)
+            q = jnp.stack(
+                [
+                    jnp.broadcast_to(rate[(s_ - 1) * XB + x, pl.ds(y + j, 1), :], (8, 128))
+                    for j in range(n)
+                ]
+            )
+            v = c_c * c + c_e * cells(src, base + x + 1, y, n)
+            v = v + (c_w * cells(src, base + x - 1, y, n) + c_n * cells(src, base + x, y + 1, n))
+            v = v + (c_s * cells(src, base + x, y - 1, n) + c_r * q)
+            v = v + (c_u * pltpu.roll(c, 127, 2) + c_l * pltpu.roll(c, 1, 2))
+            if old is not None:
+                v = v + 0.5 * cells(old, obase + x, y, n)
+            masks = []
+            if x < W:
+                masks.append(x_low)
+            if x >= W + CX:
+                masks.append(x_high)
+            if y < W:
+                masks.append(y_low)
+            if y >= W + CY:
+                masks.append(y_high)
+            if masks:
+                v = v * functools.reduce(lambda a, b: a * b, masks)
+            dst[dbase + x, pl.ds(y * 8, n * 8), :] = v.reshape(n * 8, 128)
 
     def snapshot(src, base, t):
         for fp in range(NF // 2):
@@ -282,59 +302,92 @@
                 dx, dy, side = PIECES[k][:3]
                 ok = there(-dx, -dy) if arriving else there(dx, dy)
                 if side:
-                    ok = ok & there(side, 0)
+                    ok = ok & there(side, 0) & on_chip(dy, arriving)
+                if k in FAR:
+                    ok = ok & ~on_chip(dy, arriving)
 
                 @pl.when(ok)
                 def _(k=k):
                     act(copy(par, k))
 
-        every = range(len(PIECES))
-        send = lambda c: c.start()
-        arrive = lambda c: c.wait_recv()
-        each(range(4), send, False)
-        for face, side in ((1, -1), (0, 1)):
-            each([face], arrive, True)
-            each([k for k in every if PIECES[k][2] == side], send, False)
-        each(range(2, len(PIECES)), arrive, True)
-
-        src, sbase = state, base
-        for k in range(PER):
-            r = W - 2 * k
-            stage(src, sbase, mid, 0, r - 1, coefs_1)
-            dst, dbase = (state, nxt) if k == PER - 1 else (later, (k % 2) * XB)
-            stage(mid, 0, dst, dbase, r - 2, coefs_2, src, sbase)
-            snapshot(dst, dbase, e * PER + k)
-            src, sbase = dst, dbase
-        each(every, lambda c: c.wait_send(), False)
+        def send(chosen):
+            each(chosen, lambda c: c.start(), False)
+
+        def arrive(*names):
+            each([NAMES[n] for n in names], lambda c: c.wait_recv(), True)
+
+        def held(s_):
+            if s_ % 2:
+                return mid, 0
+            if s_ in (0, W):
+                return state, (base if s_ == 0 else nxt)
+            return later, (s_ // 2 % 2) * XB
+
+        def level(i):
+            todo = []
+            for s_ in range(1, W + 1):
+                for x in range(W - (W - s_), W + CX + (W - s_)):
+                    need = max(s_ + beyond(x), 0)
+                    if need == i:
+                        todo.append((s_, x))
+            if i > 0:
+                for s_, x in todo:
+                    rates(s_, *held(s_ - 1), x)
+            done = 0
+            for s_, x in todo:
+                if i == 0 and s_ != done:
+                    for t_, z in todo:
+                        if t_ == s_:
+                            rates(s_, *held(s_ - 1), z)
+                    done = s_
+                if s_ % 2:
+                    line(s_, *held(s_ - 1), *held(s_), x, coefs_1)
+                else:
+                    line(s_, *held(s_ - 1), *held(s_), x, coefs_2, *held(s_ - 2))
+
+        pairs = [(a, b) for a in (-1, 1) for b in (-1, 1)]
+        send(range(DIRECT))
+        arrive(("y", -1), ("y", 1))
+        level(0)
+        for g in range(NEAR):
+            for dx in (-1, 1):
+                arrive(("x", g, dx))
+                send([NAMES["f", g, -dx, dy] for dy in (-1, 1)])
+        for g, (a, b) in enumerate(GROUPS):
+            if g < NEAR:
+                arrive(*[("f", g, side, dy) for side, dy in pairs])
+                arrive(*[("d", g, dx, dy) for dx, dy in pairs])
+            else:
+                arrive(("x", g, -1), ("x", g, 1), *[("d", g, dx, dy) for dx, dy in pairs])
+            for i in range(a, b + 1):
+                level(i)
+            snapshot(*held(b), e * PER + g)
+        each(range(len(PIECES)), lambda c: c.wait_send(), False)
         return 0
 
     lax.fori_loop(0, STEPS // PER, window, 0)
-
-    fetch.wait()
-    acc[...] = jnp.zeros_like(acc)
-
-    def block(kb, _):
-        fp = kb // 4
-        xp = kb % 4
-        r0 = pl.multiple_of(fp * 128 + xp * 16, 16)
-        lhs = jnp.concatenate(
-            [
-                basis[:, pl.ds(r0, 16), :].reshape(MODES * 16, 128),
-                basis[:, pl.ds(r0 + 64, 16), :].reshape(MODES * 16, 128),
-            ],
-            axis=1,
-        )
-        acc[...] += lax.dot_general(
-            lhs, snaps[kb], (((1,), (1,)), ((), ())), preferred_element_type=F32
-        )
-        return 0
-
-    lax.fori_loop(0, 16, block, 0)
 
     last = (STEPS // PER % 2) * XB
     for f in range(NF):
         for x in range(CX):
-            final_ref[f * CX + x] = state[last + W + x, pl.ds(W * 8 + f, 8, stride=8), :]
+            fields_ref[f * CX + x] = state[last + W + x, pl.ds(W * 8 + f, 8, stride=8), :]
+    keep = pltpu.make_async_copy(fields_ref, final_ref, in_sem.at[0])
+    keep.start()
+
+    fetch.wait()
+    left, right = [], []
+    for fp in range(NF // 2):
+        for xp in range(CX // 2):
+            for f in (2 * fp, 2 * fp + 1):
+                rows = basis[:, pl.ds(f * CX * CY + xp * 16, 16), :]
+                left.append(rows.reshape(MODES * 16, 128))
+            right.append(snaps[fp * 4 + xp])
+    acc[...] = lax.dot_general(
+        jnp.concatenate(left, axis=1),
+        jnp.concatenate(right, axis=1),
+        (((1,), (1,)), ((), ())),
+        preferred_element_type=F32,
+    )
 
     r16 = lax.broadcasted_iota(jnp.int32, (16, 128), 0)
     c16 = lax.broadcasted_iota(jnp.int32, (16, 128), 1)
@@ -380,6 +433,7 @@
     part[1] = total(slots_a, rank_a, na, 0)
     share(slots_b, peers_b, rank_b, nb, 1, send_b, recv_b)
     red_ref[...] = total(slots_b, rank_b, nb, 1)
+    keep.wait()
 
 
 def split3(v):
@@ -398,14 +452,17 @@
 
 
 def tail_kernel(
-    rows, red_ref, gram_ref, first_ref, second_ref, state_ref, reduced_ref, pod_ref, rhs_ref, final_ref, sem
+    rows, red_ref, gram_ref, first_ref, second_ref, state_ref, reduced_ref, pod_ref, rhs_ref, final_ref, held, sem
 ):
-    keep = pltpu.make_async_copy(state_ref, final_ref, sem)
-    keep.start()
+    bring = pltpu.make_async_copy(state_ref, held, sem.at[0])
+    bring.start()
+    keep = pltpu.make_async_copy(held, final_ref, sem.at[1])
     l = lax.axis_index("learn")
     red = red_ref[...]
     row = lax.broadcasted_iota(jnp.int32, (8, 128), 0)
     lane = lax.broadcasted_iota(jnp.int32, (8, 128), 1)
+    bring.wait()
+    keep.start()
     reduced_ref[...] = red[:, :MODES]
     pod_ref[...] = gram_ref[...] + outer_sum(red, red)[:MODES, :MODES]
     widened = jnp.where(lane == 0, 1.0, pltpu.roll(red, 1, 1))
@@ -457,12 +514,12 @@
                 jax.ShapeDtypeStruct((8, 128), F32),
             ),
             in_specs=[hbm] * 4,
-            out_specs=(vmem, vmem),
+            out_specs=(hbm, vmem),
             scratch_shapes=[
                 pltpu.VMEM((2 * XB, YB * 8, 128), F32),
                 pltpu.VMEM((XB, YB * 8, 128), F32),
                 pltpu.VMEM((2 * XB, YB * 8, 128), F32),
-                pltpu.VMEM((XB, -(-YB // 8) * 8, 128), F32),
+                pltpu.VMEM((W * XB, -(-YB // 8) * 8, 128), F32),
                 pltpu.VMEM((16, 128, 256), BF16),
                 pltpu.VMEM((MODES, NF * CX * CY, 128), BF16),
                 pltpu.VMEM((MODES * 16, 128), F32),
@@ -496,7 +553,7 @@
             ),
             in_specs=[vmem] * 4 + [hbm],
             out_specs=(vmem,) * 3 + (hbm,),
-            scratch_shapes=[pltpu.SemaphoreType.DMA],
+            scratch_shapes=[pltpu.VMEM((NF * CX, CY, 128), F32), pltpu.SemaphoreType.DMA((2,))],
             compiler_params=pltpu.CompilerParams(vmem_limit_bytes=60 * 1024 * 1024),
             name="tail",
         )(red, gram_old, jnp.asarray(first), jnp.asarray(second), final)

time: 70.9 us -> 58.3 us (0.82)
  Pallas kernels: 70.1 us -> 57.4 us
    pallas_call x1, Pallas kernels: 10.7 us -> 3.27 us  [body(): pl.pallas_call(functools.partial(tail_kernel, rows), out_shape=(jax.Shape...]
    pallas_call x1, Pallas kernels: 59.5 us -> 54.1 us  [body(): pl.pallas_call(functools.partial(steps_kernel, dims), out_shape=(jax.Shap...]
where the time goes in v2:
time: 58.3 us; the launch traced here: 58.1 us
  Pallas kernels  57.4 us (98%)
  between operations  0.64 us (1%)
    pallas_call x1, Pallas kernels, body(): pl.pallas_call(functools.partial(steps_kernel, dims), out_shape=(jax.Shap...  54.1 us
    pallas_call x1, Pallas kernels, body(): pl.pallas_call(functools.partial(tail_kernel, rows), out_shape=(jax.Shape...  3.27 us

profile of v2, /device:TPU:1, one launch (start us, length us, event | category | flops | bytes accessed | tf_op | source)
XLA Modules:
  0.0 58.1 jit_solution(2752655527998294082)
XLA Ops:
  0.6 54.1 %steps.1 = (f32[64,8,128]{2,1,0:T(8,128)}, f32[8,128]{1,0:T(8,128)}) custom-call(f32[8]{0:T(128)} %diff_hbm.1, f32[8]{0:T(128)} %stoich_hbm.1, f32[64,8,128]{2,1,0:T(8,128)} %bitcast.6, bf16[96,512,128]{2,1,0:T(8,128)(2,1)} %bitcast.5), custom_call_target="tpu_custom_call" | custom-call | tf_op jit(solution)/shard_map/steps/pallas_call | solution.py:510
  54.8 3.3 %tail.1 = (f32[8,96]{1,0:T(8,128)}, f32[96,96]{1,0:T(8,128)}, f32[96,1188]{1,0:T(8,128)}, f32[64,8,128]{2,1,0:T(8,128)}) custom-call(f32[8,128]{1,0:T(8,128)} %get-tuple-element.10.red_ref, f32[96,96]{1,0:T(8,128)} %gram_ref.1, s32[4,10,128]{2,1,0:T(8,128)} %constant.4.clone.first_ref, s32[4,10,128]{2,1,0:T(8,128)} %constant.5.clone.second_ref, ...), custom_call_target="tpu_custom_call" | custom-call | tf_op jit(solution)/shard_map/tail/pallas_call | solution.py:546

commit v3 on v2

--- a/solution.py
+++ b/solution.py
@@ -361,7 +361,8 @@
                 arrive(("x", g, -1), ("x", g, 1), *[("d", g, dx, dy) for dx, dy in pairs])
             for i in range(a, b + 1):
                 level(i)
-            snapshot(*held(b), e * PER + g)
+                if i % 2 == 0:
+                    snapshot(*held(i), e * PER + i // 2 - 1)
         each(range(len(PIECES)), lambda c: c.wait_send(), False)
         return 0
 
@@ -452,17 +453,14 @@
 
 
 def tail_kernel(
-    rows, red_ref, gram_ref, first_ref, second_ref, state_ref, reduced_ref, pod_ref, rhs_ref, final_ref, held, sem
+    rows, red_ref, gram_ref, first_ref, second_ref, state_ref, reduced_ref, pod_ref, rhs_ref, final_ref, sem
 ):
-    bring = pltpu.make_async_copy(state_ref, held, sem.at[0])
-    bring.start()
-    keep = pltpu.make_async_copy(held, final_ref, sem.at[1])
+    keep = pltpu.make_async_copy(state_ref, final_ref, sem)
+    keep.start()
     l = lax.axis_index("learn")
     red = red_ref[...]
     row = lax.broadcasted_iota(jnp.int32, (8, 128), 0)
     lane = lax.broadcasted_iota(jnp.int32, (8, 128), 1)
-    bring.wait()
-    keep.start()
     reduced_ref[...] = red[:, :MODES]
     pod_ref[...] = gram_ref[...] + outer_sum(red, red)[:MODES, :MODES]
     widened = jnp.where(lane == 0, 1.0, pltpu.roll(red, 1, 1))
@@ -551,9 +549,9 @@
                 jax.ShapeDtypeStruct((MODES, rows), F32),
                 jax.ShapeDtypeStruct((NF * CX, CY, 128), F32),
             ),
-            in_specs=[vmem] * 4 + [hbm],
+            in_specs=[vmem] * 5,
             out_specs=(vmem,) * 3 + (hbm,),
-            scratch_shapes=[pltpu.VMEM((NF * CX, CY, 128), F32), pltpu.SemaphoreType.DMA((2,))],
+            scratch_shapes=[pltpu.SemaphoreType.DMA],
             compiler_params=pltpu.CompilerParams(vmem_limit_bytes=60 * 1024 * 1024),
             name="tail",
         )(red, gram_old, jnp.asarray(first), jnp.asarray(second), final)

time: 58.3 us -> 57.5 us (0.986)
  Pallas kernels: 57.4 us -> 56.7 us
    pallas_call x1, Pallas kernels: 3.27 us -> 2.54 us  [body(): pl.pallas_call(functools.partial(tail_kernel, rows), out_shape=(jax.Shape...]
where the time goes in v3:
time: 57.5 us; the launch traced here: 57.3 us
  Pallas kernels  56.7 us (99%)
  between operations  0.64 us (1%)
    pallas_call x1, Pallas kernels, body(): pl.pallas_call(functools.partial(steps_kernel, dims), out_shape=(jax.Shap...  54.1 us
    pallas_call x1, Pallas kernels, body(): pl.pallas_call(functools.partial(tail_kernel, rows), out_shape=(jax.Shape...  2.54 us

profile of v3, /device:TPU:1, one launch (start us, length us, event | category | flops | bytes accessed | tf_op | source)
XLA Modules:
  0.0 57.3 jit_solution(5632340100781961189)
XLA Ops:
  0.6 54.1 %steps.1 = (f32[64,8,128]{2,1,0:T(8,128)}, f32[8,128]{1,0:T(8,128)}) custom-call(f32[8]{0:T(128)} %diff_hbm.1, f32[8]{0:T(128)} %stoich_hbm.1, f32[64,8,128]{2,1,0:T(8,128)} %bitcast.6, bf16[96,512,128]{2,1,0:T(8,128)(2,1)} %bitcast.5), custom_call_target="tpu_custom_call" | custom-call | tf_op jit(solution)/shard_map/steps/pallas_call | solution.py:508
  54.8 2.5 %tail.1 = (f32[8,96]{1,0:T(8,128)}, f32[96,96]{1,0:T(8,128)}, f32[96,1188]{1,0:T(8,128)}, f32[64,8,128]{2,1,0:T(8,128)}) custom-call(f32[8,128]{1,0:T(8,128)} %get-tuple-element.10.red_ref, f32[96,96]{1,0:T(8,128)} %gram_ref.1, s32[4,10,128]{2,1,0:T(8,128)} %constant.4.clone.first_ref, s32[4,10,128]{2,1,0:T(8,128)} %constant.5.clone.second_ref, ...), custom_call_target="tpu_custom_call" | custom-call | tf_op jit(solution)/shard_map/tail/pallas_call | solution.py:544

commit v4 on v3

--- a/solution.py
+++ b/solution.py
@@ -109,29 +109,6 @@
     l = lax.axis_index("learn")
 
     fetch = pltpu.make_async_copy(basis_ref, basis, basis_sem)
-    loads = [
-        pltpu.make_async_copy(a, b, in_sem.at[i])
-        for i, (a, b) in enumerate(
-            ((fields_hbm, fields_ref), (diff_hbm, diff_ref), (stoich_hbm, stoich_ref))
-        )
-    ]
-    for c in loads:
-        c.start()
-    fetch.start()
-
-    for par in range(2):
-        for edge, x in ((s == 0, par * XB), (s == lax.axis_size("sim") - 1, par * XB + W + CX)):
-
-            @pl.when(edge)
-            def _(x=x):
-                state[pl.ds(x, W)] = jnp.zeros((W, YB * 8, 128), F32)
-
-        for edge, y in ((l == 0, 0), (l == lax.axis_size("learn") - 1, W + CY)):
-
-            @pl.when(edge)
-            def _(par=par, y=y):
-                state[pl.ds(par * XB, XB), pl.ds(y * 8, W * 8), :] = jnp.zeros((XB, W * 8, 128), F32)
-
     x_me = s % x_n
     z_me = (s // x_n) % z_n
     yh_me = s // (x_n * z_n)
@@ -178,6 +155,29 @@
 
     for ps, pl_ in peers_a + peers_b:
         pl.semaphore_signal(barrier, inc=1, device_id={"sim": ps, "learn": pl_}, device_id_type=MESH)
+
+    loads = [
+        pltpu.make_async_copy(a, b, in_sem.at[i])
+        for i, (a, b) in enumerate(
+            ((fields_hbm, fields_ref), (diff_hbm, diff_ref), (stoich_hbm, stoich_ref))
+        )
+    ]
+    for c in loads:
+        c.start()
+    fetch.start()
+
+    for par in range(2):
+        for edge, x in ((s == 0, par * XB), (s == lax.axis_size("sim") - 1, par * XB + W + CX)):
+
+            @pl.when(edge)
+            def _(x=x):
+                state[pl.ds(x, W)] = jnp.zeros((W, YB * 8, 128), F32)
+
+        for edge, y in ((l == 0, 0), (l == lax.axis_size("learn") - 1, W + CY)):
+
+            @pl.when(edge)
+            def _(par=par, y=y):
+                state[pl.ds(par * XB, XB), pl.ds(y * 8, W * 8), :] = jnp.zeros((XB, W * 8, 128), F32)
 
     for c in loads:
         c.wait()
@@ -292,29 +292,29 @@
 
     pl.semaphore_wait(barrier, count)
 
+    def each(par, chosen, act, arriving):
+        for k in chosen:
+            dx, dy, side = PIECES[k][:3]
+            ok = there(-dx, -dy) if arriving else there(dx, dy)
+            if side:
+                ok = ok & there(side, 0) & on_chip(dy, arriving)
+            if k in FAR:
+                ok = ok & ~on_chip(dy, arriving)
+
+            @pl.when(ok)
+            def _(k=k):
+                act(copy(par, k))
+
     def window(e, _):
         par = lax.rem(e, 2)
         base = par * XB
         nxt = (1 - par) * XB
 
-        def each(chosen, act, arriving):
-            for k in chosen:
-                dx, dy, side = PIECES[k][:3]
-                ok = there(-dx, -dy) if arriving else there(dx, dy)
-                if side:
-                    ok = ok & there(side, 0) & on_chip(dy, arriving)
-                if k in FAR:
-                    ok = ok & ~on_chip(dy, arriving)
-
-                @pl.when(ok)
-                def _(k=k):
-                    act(copy(par, k))
-
         def send(chosen):
-            each(chosen, lambda c: c.start(), False)
+            each(par, chosen, lambda c: c.start(), False)
 
         def arrive(*names):
-            each([NAMES[n] for n in names], lambda c: c.wait_recv(), True)
+            each(par, [NAMES[n] for n in names], lambda c: c.wait_recv(), True)
 
         def held(s_):
             if s_ % 2:
@@ -346,7 +346,6 @@
                     line(s_, *held(s_ - 1), *held(s_), x, coefs_2, *held(s_ - 2))
 
         pairs = [(a, b) for a in (-1, 1) for b in (-1, 1)]
-        send(range(DIRECT))
         arrive(("y", -1), ("y", 1))
         level(0)
         for g in range(NEAR):
@@ -361,11 +360,18 @@
                 arrive(("x", g, -1), ("x", g, 1), *[("d", g, dx, dy) for dx, dy in pairs])
             for i in range(a, b + 1):
                 level(i)
+                if i == W:
+
+                    @pl.when(e < STEPS // PER - 1)
+                    def _():
+                        each(1 - par, range(DIRECT), lambda c: c.start(), False)
+
                 if i % 2 == 0:
                     snapshot(*held(i), e * PER + i // 2 - 1)
-        each(range(len(PIECES)), lambda c: c.wait_send(), False)
+        each(par, range(len(PIECES)), lambda c: c.wait_send(), False)
         return 0
 
+    each(0, range(DIRECT), lambda c: c.start(), False)
     lax.fori_loop(0, STEPS // PER, window, 0)
 
     last = (STEPS // PER % 2) * XB
@@ -397,10 +403,9 @@
     kept = jnp.concatenate([kept, jnp.zeros((128 - MODES, 128), F32)], axis=0)
     groups = (lane // 16 == row).astype(F32)
     mine = lax.dot_general(
-        groups,
-        kept,
+        jnp.concatenate([groups] * 3, axis=1).astype(BF16),
+        jnp.concatenate(split3(kept), axis=1).astype(BF16),
         (((1,), (1,)), ((), ())),
-        precision=lax.Precision.HIGHEST,
         preferred_element_type=F32,
     )
 

time: 57.5 us -> 57.2 us (level)
  no operation moved by 1% of the time
where the time goes in v4:
time: 57.2 us; the launch traced here: 57.1 us
  Pallas kernels  56.5 us (99%)
  between operations  0.64 us (1%)
    pallas_call x1, Pallas kernels, body(): pl.pallas_call(functools.partial(steps_kernel, dims), out_shape=(jax.Shap...  53.9 us
    pallas_call x1, Pallas kernels, body(): pl.pallas_call(functools.partial(tail_kernel, rows), out_shape=(jax.Shape...  2.54 us

profile of v4, /device:TPU:1, one launch (start us, length us, event | category | flops | bytes accessed | tf_op | source)
XLA Modules:
  0.0 57.1 jit_solution(10994596044469736091)
XLA Ops:
  0.6 53.9 %steps.1 = (f32[64,8,128]{2,1,0:T(8,128)}, f32[8,128]{1,0:T(8,128)}) custom-call(f32[8]{0:T(128)} %diff_hbm.1, f32[8]{0:T(128)} %stoich_hbm.1, f32[64,8,128]{2,1,0:T(8,128)} %bitcast.6, bf16[96,512,128]{2,1,0:T(8,128)(2,1)} %bitcast.5), custom_call_target="tpu_custom_call" | custom-call | tf_op jit(solution)/shard_map/steps/pallas_call | solution.py:513
  54.6 2.5 %tail.1 = (f32[8,96]{1,0:T(8,128)}, f32[96,96]{1,0:T(8,128)}, f32[96,1188]{1,0:T(8,128)}, f32[64,8,128]{2,1,0:T(8,128)}) custom-call(f32[8,128]{1,0:T(8,128)} %get-tuple-element.10.red_ref, f32[96,96]{1,0:T(8,128)} %gram_ref.1, s32[4,10,128]{2,1,0:T(8,128)} %constant.4.clone.first_ref, s32[4,10,128]{2,1,0:T(8,128)} %constant.5.clone.second_ref, ...), custom_call_target="tpu_custom_call" | custom-call | tf_op jit(solution)/shard_map/tail/pallas_call | solution.py:549

commit v5 on v4

--- a/solution.py
+++ b/solution.py
@@ -458,7 +458,7 @@
 
 
 def tail_kernel(
-    rows, red_ref, gram_ref, first_ref, second_ref, state_ref, reduced_ref, pod_ref, rhs_ref, final_ref, sem
+    rows, red_ref, gram_ref, tables_ref, state_ref, reduced_ref, pod_ref, rhs_ref, final_ref, sem
 ):
     keep = pltpu.make_async_copy(state_ref, final_ref, sem)
     keep.start()
@@ -471,9 +471,9 @@
     widened = jnp.where(lane == 0, 1.0, pltpu.roll(red, 1, 1))
     changes = jnp.where(row < STEPS - 1, pltpu.roll(red, 7, 0) - red, 0.0)
     feats = []
-    for j in range(first_ref.shape[1]):
-        one = jnp.broadcast_to(first_ref[l, pl.ds(j, 1), :], (8, 128))
-        two = jnp.broadcast_to(second_ref[l, pl.ds(j, 1), :], (8, 128))
+    for j in range(tables_ref.shape[2]):
+        one = jnp.broadcast_to(tables_ref[0, l, pl.ds(j, 1), :], (8, 128))
+        two = jnp.broadcast_to(tables_ref[1, l, pl.ds(j, 1), :], (8, 128))
         feats.append(
             jnp.take_along_axis(widened, one, axis=1, mode="promise_in_bounds")
             * jnp.take_along_axis(widened, two, axis=1, mode="promise_in_bounds")
@@ -554,12 +554,12 @@
                 jax.ShapeDtypeStruct((MODES, rows), F32),
                 jax.ShapeDtypeStruct((NF * CX, CY, 128), F32),
             ),
-            in_specs=[vmem] * 5,
+            in_specs=[vmem] * 4,
             out_specs=(vmem,) * 3 + (hbm,),
             scratch_shapes=[pltpu.SemaphoreType.DMA],
             compiler_params=pltpu.CompilerParams(vmem_limit_bytes=60 * 1024 * 1024),
             name="tail",
-        )(red, gram_old, jnp.asarray(first), jnp.asarray(second), final)
+        )(red, gram_old, jnp.asarray(np.stack([first, second])), final)
         return final.reshape(NF, CX, CY, 128), reduced.T, pod, rhs.T
 
     in_specs = (

time: 57.2 us -> 57.2 us (level)
  no operation moved by 1% of the time
where the time goes in v5:
time: 57.2 us; the launch traced here: 57.1 us
  Pallas kernels  56.5 us (99%)
  between operations  0.64 us (1%)
    pallas_call x1, Pallas kernels, body(): pl.pallas_call(functools.partial(steps_kernel, dims), out_shape=(jax.Shap...  53.9 us
    pallas_call x1, Pallas kernels, body(): pl.pallas_call(functools.partial(tail_kernel, rows), out_shape=(jax.Shape...  2.54 us

profile of v5, /device:TPU:1, one launch (start us, length us, event | category | flops | bytes accessed | tf_op | source)
XLA Modules:
  0.0 57.1 jit_solution(17654418968538149543)
XLA Ops:
  0.6 53.9 %steps.1 = (f32[64,8,128]{2,1,0:T(8,128)}, f32[8,128]{1,0:T(8,128)}) custom-call(f32[8]{0:T(128)} %diff_hbm.1, f32[8]{0:T(128)} %stoich_hbm.1, f32[64,8,128]{2,1,0:T(8,128)} %bitcast.6, bf16[96,512,128]{2,1,0:T(8,128)(2,1)} %bitcast.5), custom_call_target="tpu_custom_call" | custom-call | tf_op jit(solution)/shard_map/steps/pallas_call | solution.py:513
  54.6 2.5 %tail.1 = (f32[8,96]{1,0:T(8,128)}, f32[96,96]{1,0:T(8,128)}, f32[96,1188]{1,0:T(8,128)}, f32[64,8,128]{2,1,0:T(8,128)}) custom-call(f32[8,128]{1,0:T(8,128)} %get-tuple-element.10.red_ref, f32[96,96]{1,0:T(8,128)} %gram_ref.1, s32[2,4,10,128]{3,2,1,0:T(8,128)} %constant.2.clone.tables_ref, f32[64,8,128]{2,1,0:T(8,128)} %get-tuple-element.11.state_ref), custom_call_target="tpu_custom_call" | custom-call | tf_op jit(solution)/shard_map/tail/pallas_call | solution.py:549
